TPU v7x, 128 devices: a whole 4x4x4 slice. The times are simulated.
128 devices in a mesh: group: 4 (over y), queue: 32 (over z, x, core).
Axes of the slice: x: 4, y: 4, z: 4, core: 2. Of those that a mesh axis runs over, the one named last changes fastest.
Arguments:
- queries: bfloat16 [32, 64, 128], P('queue', 'group'), may hold values from -4 to 4
- positive: int32 [64], replicated, may hold values from 0 to 16383
- queue: bfloat16 [16384, 96, 128], P(('group', 'queue')), may hold values from -4 to 4
- slot_order: int32 [16384], P(('group', 'queue')), may hold values from 0 to 16383, each once
Outputs:
- loss: float32 [], replicated
- query_grad: float32 [32, 64, 128], P('queue', 'group')
Inputs may be any that keep to these rules, and one draw needn't show every extreme that they name: `slot_order`: every id of 0 to 16383 stands in exactly one slot.
All inputs are finite; a program needn't handle non-finite values.
Results may differ from a plain program's by a relative error of at most 0.017.
Values may be sent and summed in bfloat16 or wider, within the bound.
A program may use at most 64 MiB of HBM per device.

v0:
```python
import jax
import jax.numpy as jnp
from jax import lax
from jax.sharding import PartitionSpec as P

sharpness = 0.1
softness_divisor = 0.05
epsilon = 1e-06


def unit_vectors(values):
    wide = values.astype(jnp.float32)
    length = jnp.sqrt(jnp.sum(wide * wide, axis=-1, keepdims=True) + epsilon)
    return (wide / length, length)


def token_terms(query_block, documents):
    dots = jnp.einsum("tbk,djk->tbjd", query_block, documents, preferred_element_type=jnp.float32)
    powered = jnp.exp(dots / sharpness)
    return (powered, jnp.sum(powered, axis=2))


def block_length():
    return 2


def score_sum(query_all, documents):
    token_count = query_all.shape[0]
    step_len = block_length()

    def score_add_tokens(step_index, similarity_scores):
        query_block = lax.dynamic_slice_in_dim(query_all, step_index * step_len, step_len, 0)
        powered, summed = token_terms(query_block, documents)
        return similarity_scores + jnp.sum(sharpness * jnp.log(summed), axis=0)

    empty = jnp.zeros((query_all.shape[1], documents.shape[0]), jnp.float32)
    return lax.fori_loop(0, token_count // step_len, score_add_tokens, empty)


def token_gradient(query_matrix, documents, softmax_factor):
    token_count = query_matrix.shape[0]
    step_len = block_length()

    def token_add_tokens(step_index, grads):
        query_block = lax.dynamic_slice_in_dim(query_matrix, step_index * step_len, step_len, 0)
        powered, summed = token_terms(query_block, documents)
        weights = (softmax_factor[None, :, None, :] * powered / summed[:, :, None, :]).astype(
            jnp.bfloat16
        )
        contrib = jnp.einsum(
            "tbjd,djk->tbk", weights, documents, preferred_element_type=jnp.float32
        )
        return lax.dynamic_update_slice_in_dim(grads, contrib, step_index * step_len, 0)

    empty = jnp.zeros((token_count, query_matrix.shape[1], documents.shape[2]), jnp.float32)
    return lax.fori_loop(0, token_count // step_len, token_add_tokens, empty)


def on_device(queries, positive, queue, slot_order):
    query_unit, query_length = unit_vectors(queries)
    query_half = query_unit.astype(jnp.bfloat16)
    all_tokens = lax.all_gather(query_half, "queue", axis=0, tiled=True)
    query_all = lax.all_gather(all_tokens, "group", axis=1, tiled=True)
    doc_half = unit_vectors(queue)[0].astype(jnp.bfloat16)
    similarity_scores = score_sum(query_all, doc_half)
    scaled_logits = similarity_scores / softness_divisor
    positive_match = slot_order[None, :] == positive[:, None]
    local_target = jnp.sum(jnp.where(positive_match, scaled_logits, 0.0), axis=1)
    local_top = jnp.max(scaled_logits, axis=1)
    top = lax.pmax(local_top, ("group", "queue"))
    local_total = jnp.sum(jnp.exp(scaled_logits - top[:, None]), axis=1)
    total, target = lax.psum((local_total, local_target), ("group", "queue"))
    log_partition = top + jnp.log(total)
    loss = jnp.mean(log_partition - target)
    softmax_factor = (
        jnp.exp(scaled_logits - log_partition[:, None]) - positive_match.astype(jnp.float32)
    ) / softness_divisor
    own_tokens = queries.shape[0]
    own_rows = queries.shape[1]
    every_term = token_gradient(query_all, doc_half, softmax_factor)
    summed = lax.psum(every_term, ("group", "queue"))
    token_slice = lax.dynamic_slice_in_dim(
        summed, lax.axis_index("queue") * own_tokens, own_tokens, 0
    )
    unit_grad = lax.dynamic_slice_in_dim(
        token_slice, lax.axis_index("group") * own_rows, own_rows, 1
    )
    query_grad = (
        unit_grad - query_unit * jnp.sum(query_unit * unit_grad, axis=-1, keepdims=True)
    ) / query_length
    return (loss, query_grad)


def solution(mesh):
    return jax.shard_map(
        on_device,
        mesh=mesh,
        in_specs=(
            P("queue", "group", None),
            P(),
            P(("group", "queue"), None, None),
            P(("group", "queue")),
        ),
        out_specs=(P(), P("queue", "group", None)),
        check_vma=False,
    )
```

profile of v0, /device:TPU:1, one launch (start us, length us, event | category | flops | bytes accessed | tf_op | source)
XLA Modules:
  0.0 437.0 jit_solution(12951355894353039478)
XLA Ops:
  8.8 27.2 %all_gather.6 = bf16[32,16,128]{2,1,0:T(8,128)(2,1)S(1)} all-gather(bf16[1,16,128]{2,1,0:T(8,128)(2,1)S(1)} %fusion.34), channel_id=1, replica_groups=mesh['group'=4,'queue'=32] {'queue'}, dimensions={0}, use_global_device_ids=true | all-gather | bytes 135168 | tf_op jit(solution)/shard_map/all_gather | solution.py:62
  36.0 11.6 %all_gather.7 = bf16[32,64,128]{2,1,0:T(8,128)(2,1)} all-gather(bf16[32,16,128]{2,1,0:T(8,128)(2,1)S(1)} %all_gather.6), channel_id=1, replica_groups=mesh['group'=4,'queue'=32] {'group'}, dimensions={1}, use_global_device_ids=true | all-gather | bytes 655360 | tf_op jit(solution)/shard_map/all_gather | solution.py:63
  47.6 3.6 fusion.28
  51.2 4.6 %fusion.29 = bf16[128,96,128]{2,0,1:T(8,128)(2,1)S(1)} fusion(f32[128,96]{0,1:T(8,128)S(1)} %add_sqrt_fusion, bf16[128,96,128]{2,1,0:T(8,128)(2,1)} %param.10), kind=kLoop, calls=%fused_computation.26 | loop fusion | flops 4718592 | bytes 6340608 | tf_op jit(solution)/shard_map/convert_element_type | solution.py:64
  55.8 29.7 %while.28 = (s32[]{:T(128)}, f32[64,128]{1,0:T(8,128)S(1)}, bf16[32,64,128]{2,1,0:T(8,128)(2,1)}, bf16[128,96,128]{2,0,1:T(8,128)(2,1)S(1)}, s32[]{:T(128)}, /*index=5*/s32[]{:T(128)}, s32[]{:T(128)}, s32[]{:T(128)}) while((s32[]{:T(128)}, f32[64,128]{1,0:T(8,128)S(1)}, bf16[32,64,128]{2,1,0:T(8,128)(2,1)}, ...), condition=%wide.region_5.0_spmd.clone, body=%wide.region_2.0_spmd.clone.sunk | while | flops 405823488 | bytes 3440793 | solution.py:37
  85.6 66.5 %pmax.7 = f32[64]{0:T(128)S(1)} all-reduce(f32[64]{0:T(128)S(1)} %multiply_reduce_fusion.1), channel_id=1, replica_groups=mesh['group'=4,'queue'=32] {'group','queue'}, use_global_device_ids=true, to_apply=%region_7.8 | all-reduce | flops 64 | bytes 512 | tf_op jit(solution)/shard_map/pmax | solution.py:70
  152.3 62.5 %all-reduce = (f32[64]{0:T(128)S(1)}, f32[64]{0:T(128)S(1)}) all-reduce(f32[64]{0:T(128)S(1)} %get-tuple-element.193, f32[64]{0:T(128)S(1)} %get-tuple-element.192), channel_id=1, replica_groups=mesh['group'=4,'queue'=32] {'group','queue'}, use_global_device_ids=true, to_apply=%region_9.10 | all-reduce | flops 128 | bytes 1024 | tf_op jit(solution)/shard_map/psum | solution.py:72
  216.6 65.5 %while.27 = (s32[]{:T(128)}, f32[32,64,128]{2,1,0:T(8,128)}, f32[64,128]{1,0:T(8,128)S(1)}, bf16[32,64,128]{2,1,0:T(8,128)(2,1)}, bf16[128,96,128]{2,0,1:T(8,128...) while((s32[]{:T(128)}, f32[32,64,128]{2,1,0:T(8,128)}, f32[64,128]{1,0:T(8,128)S(1)}, ...), condition=%wide.region_15.16_spmd, body=%wide.region_13.15_spmd.sunk | while | flops 814727168 | bytes 19136668 | solution.py:56
  218.4 2.3 fusion.42
  222.5 2.3 fusion.42
  226.6 2.3 fusion.42
  230.7 2.3 fusion.42
  238.9 2.3 fusion.42
  243.0 2.3 fusion.42
  247.1 2.3 fusion.42
  251.2 2.3 fusion.42
  255.3 2.3 fusion.42
  259.4 2.3 fusion.42
  263.5 2.3 fusion.42
  267.6 2.3 fusion.42
  271.7 2.3 fusion.42
  275.7 2.3 fusion.42
  279.8 2.3 fusion.42
  282.8 144.0 %all-reduce.3.cloned.1.call-done = f32[32,64,128]{2,1,0:T(8,128)} async-done(((f32[32,64,128]{2,1,0:T(8,128)}), f32[32,64,128]{2,1,0:T(8,128)}) %all-reduce.3.cloned.1.call-update) | async-done | bytes 1048592 | tf_op jit(solution)/shard_map/psum | solution.py:81
  (85 shorter events, 66.4 us)
Async XLA Ops:
  7.2 419.6 %all-reduce.3.cloned.1.call-start = ((), (), s32[]{:S(2)}) async-start(), calls=%async_computation | async-start | bytes 2097152 | tf_op jit(solution)/shard_map/psum | solution.py:81
  55.8 96.3 %copy-start.1 = (s32[128]{0:T(128)S(1)}, s32[128]{0:T(128)}, u32[]{:S(2)}) copy-start(s32[128]{0:T(128)} %param.11) | copy-start | bytes 1540
  55.8 96.3 %copy-start.2 = (s32[64]{0:T(128)S(1)}, s32[64]{0:T(128)}, u32[]{:S(2)}) copy-start(s32[64]{0:T(128)} %param.9) | copy-start | bytes 772
  216.6 210.2 %copy-start = (bf16[1,16,128]{2,1,0:T(8,128)(2,1)S(1)}, bf16[1,16,128]{2,1,0:T(8,128)(2,1)}, u32[]{:S(2)}) copy-start(bf16[1,16,128]{2,1,0:T(8,128)(2,1)} %param.8) | copy-start | bytes 12292
Sparse Core Ops, SparseCore 0:
  282.3 144.4 all-reduce.2
where the time goes:
time: 440 us; the launch traced here: 437 us
  blocking collectives  168 us (38%)
  waiting for transfers between devices  144 us (33%)
  matrix products  93.9 us (21%)
  between operations  15.9 us (4%)
  other arithmetic  13.5 us (3%)
    psum x1, waiting for transfers between devices, on_device(): summed = lax.psum(every_term, ('group', 'queue'))  144 us
    pmax x1, blocking collectives, on_device(): top = lax.pmax(local_top, ('group', 'queue'))  66.5 us
    psum x1, blocking collectives, on_device(): total, target = lax.psum((local_total, local_target), ('group', 'queue'))  62.5 us
    dot_general x32, matrix products, token_terms(): jnp.einsum('tbk,djk->tbjd', query_block, documents, preferred_element_typ...  57.7 us
    dot_general x16, matrix products, token_add_tokens(): jnp.einsum('tbjd,djk->tbk', weights, documents, preferred_element_type=jn...  36.3 us
    all_gather x1, blocking collectives, on_device(): all_tokens = lax.all_gather(query_half, 'queue', axis=0, tiled=True)  27.2 us
    all_gather x1, blocking collectives, on_device(): query_all = lax.all_gather(all_tokens, 'group', axis=1, tiled=True)  11.6 us
  transfers between devices with their start and end apart: 1, of which 1 were waited for; matrix products, arithmetic and copies ran while one was open for 0% of the time, Pallas kernels for 0%

commit v1 on v0

v1 whole, which is shorter than its diff:
```python
import functools

import jax
import jax.numpy as jnp
from jax import lax
from jax.experimental import pallas as pl
from jax.experimental.pallas import tpu as pltpu
from jax.sharding import PartitionSpec as P

sharpness = 0.1
softness_divisor = 0.05
epsilon = 1e-06
log2e = 1.4426950408889634
MESH = pl.DeviceIdType.MESH
ROWS = 16
HALF = 8


def first_order(k, group):
    own = lax.div(4 - k, 4)
    other = (k - 1) + lax.div(k + 3 - group, 4)
    return own * group + (1 - own) * other


def last_order(k, group, groups):
    own = lax.div(k, groups - 1)
    other = k + lax.div(k - group + 4, 4)
    return own * group + (1 - own) * other


def kernel(
    groups, tokens, docs, length, chunks, vmem,
    pos_ref, q_ref, slot_ref, queue_ref,
    grad_ref, loss_ref,
    powered, doc, doc_t, qbuf, sums, logits, coef, slot_col, st1, st2, fin, gsend, grecv, yrecv, partial,
    load_sem, qy_recv, q_recv, s1_recv, s2_recv, g_recv, y_recv, send_sem,
):
    group = lax.axis_index("group")
    me = lax.axis_index("queue")
    rows = docs * length
    lanes = HALF * tokens
    chunk = rows // chunks
    blocks = 4
    block_rows = rows // blocks

    def load(c):
        part = pl.ds(c * chunk, chunk)
        return pltpu.make_async_copy(queue_ref.at[part], doc.at[part], load_sem.at[c])

    for c in range(chunks):
        load(c).start()

    def peer_of(j):
        return lax.rem(me + j, tokens)

    def other_group(j):
        return lax.rem(group + j, groups)

    barrier = pltpu.get_barrier_semaphore()

    def greet(j, carry):
        pl.semaphore_signal(barrier, inc=1, device_id={"queue": peer_of(j)}, device_id_type=MESH)
        return carry

    lax.fori_loop(1, tokens, greet, 0)
    for j in range(1, groups):
        pl.semaphore_signal(barrier, inc=1, device_id={"group": other_group(j)}, device_id_type=MESH)

    wide = q_ref[...].astype(jnp.float32)
    q_length = jnp.sqrt(jnp.sum(wide * wide, axis=-1, keepdims=True) + epsilon)
    q_unit = wide / q_length
    qbuf[group * tokens + me] = q_unit.astype(jnp.bfloat16)
    slot_col[...] = jnp.broadcast_to(slot_ref[...].astype(jnp.float32), (128, docs)).T

    pl.semaphore_wait(barrier, tokens - 1 + groups - 1)

    def to_group(src, dst, send, recv, j):
        return pltpu.make_async_remote_copy(
            src_ref=src, dst_ref=dst, send_sem=send, recv_sem=recv,
            device_id={"group": j}, device_id_type=MESH,
        )

    def to_peer(src, dst, send, recv, j):
        return pltpu.make_async_remote_copy(
            src_ref=src, dst_ref=dst, send_sem=send, recv_sem=recv,
            device_id={"queue": j}, device_id_type=MESH,
        )

    def wait_in(ref, sem):
        to_peer(ref, ref, send_sem.at[0], sem, me).wait_recv()

    def wait_out(ref, sem):
        to_peer(ref, ref, sem, q_recv.at[0], me).wait_send()

    mine = qbuf.at[group * tokens + me]
    for j in range(1, groups):
        to_group(mine, mine, send_sem.at[0], qy_recv.at[group], other_group(j)).start()

    def spread(g):
        block = qbuf.at[g * tokens + me]

        def body(j, carry):
            to_peer(block, block, send_sem.at[0], q_recv.at[g], peer_of(j)).start()
            return carry

        lax.fori_loop(1, tokens, body, 0)

    spread(group)

    def normalize(c):
        load(c).wait()
        part = pl.ds(c * chunk, chunk)
        x = doc[part, :].astype(jnp.float32)
        y = x * lax.rsqrt(jnp.sum(x * x, axis=-1, keepdims=True) + epsilon)
        doc[part, :] = y.astype(jnp.bfloat16)
        doc_t[:, part] = y.T.astype(jnp.bfloat16)

    def pass_on(j):
        g = other_group(j)
        block = qbuf.at[g * tokens + me]
        wait_in(block, qy_recv.at[g])
        spread(g)

    for c in range(chunks):
        normalize(c)
        if c == chunks // 2:
            for j in range(1, groups):
                pass_on(j)

    lane = lax.broadcasted_iota(jnp.int32, (1, 128), 1)
    lane = lax.rem(lane, HALF)

    def hits(t):
        wanted = jnp.zeros((1, 128), jnp.float32)
        for b in range(HALF):
            wanted = jnp.where(lane == b, pos_ref[t * HALF + b].astype(jnp.float32), wanted)
        return slot_col[...] == wanted

    def score_tile(g, h):
        t = g * 2 + h
        q = qbuf[pl.ds(g * tokens, tokens)].astype(jnp.float32)
        q = jnp.where(h == 0, q[:, :HALF], q[:, HALF:])
        q = q.reshape(lanes, 128).T.astype(jnp.bfloat16)
        for c in range(blocks):
            part = pl.ds(c * block_rows, block_rows)
            x = jnp.dot(doc[part, :], q, preferred_element_type=jnp.float32)
            e = jnp.exp2(x * (log2e / sharpness))
            powered[t, part, :] = e.astype(jnp.bfloat16)
            summed = jnp.sum(e.reshape(docs // blocks, length, lanes), axis=1)
            sums[t, c * (docs // blocks):(c + 1) * (docs // blocks), :] = summed
        score = jnp.log(sums[t]) * (sharpness / softness_divisor)
        total = score[:, :128]
        for c in range(1, lanes // 128):
            total = total + score[:, c * 128:(c + 1) * 128]
        for shift in (8, 16, 32, 64):
            total = total + pltpu.roll(total, shift, 1)
        logits[t] = total
        top = jnp.max(total, axis=0, keepdims=True)
        row = g * tokens + me
        st1[row, pl.ds(h, 1), :] = top
        st1[row, pl.ds(4 + h, 1), :] = jnp.sum(jnp.exp(total - top), axis=0, keepdims=True)
        st1[row, pl.ds(6 + h, 1), :] = jnp.sum(jnp.where(hits(t), total, 0.0), axis=0, keepdims=True)

    def combine(parts):
        top = jnp.max(parts, axis=0)
        scale = jnp.exp(pltpu.roll(parts, 4, 1) - pltpu.roll(top, 4, 0)[None])
        row = lax.broadcasted_iota(jnp.int32, (8, 128), 0)
        return jnp.where(row < 4, top, jnp.sum(parts * scale, axis=0))

    def send_stats(g):
        block = st1.at[g * tokens + me]

        def body(j, carry):
            to_peer(block, block, send_sem.at[1], s1_recv.at[g], peer_of(j)).start()
            return carry

        lax.fori_loop(1, tokens, body, 0)

    def combine_plane(g):
        wait_in(st1.at[pl.ds(0, tokens - 1)], s1_recv.at[g])
        block = st2.at[g * groups + group]
        st2[g * groups + group] = combine(st1[pl.ds(g * tokens, tokens)])
        for j in range(1, groups):
            to_group(block, block, send_sem.at[2], s2_recv.at[g], other_group(j)).start()

    def combine_groups(g):
        wait_in(st2.at[pl.ds(0, groups - 1)], s2_recv.at[g])
        fin[g] = combine(st2[pl.ds(g * groups, groups)])

    def pass_a(k, carry):
        g = first_order(k, group)

        @pl.when(k > 0)
        def _():
            wait_in(qbuf.at[pl.ds(0, tokens - 1)], q_recv.at[g])

        def tile(h, c):
            score_tile(g, h)
            return c

        lax.fori_loop(0, 2, tile, 0)
        send_stats(g)

        @pl.when(k > 0)
        def _():
            combine_plane(first_order(k - 1, group))

        return carry

    wait_in(qbuf.at[pl.ds(0, tokens - 1)], q_recv.at[group])
    zero = jnp.zeros((2, 128), jnp.float32)

    def clear(g, carry):
        st1[g * tokens + me, 2:4, :] = zero
        return carry

    lax.fori_loop(0, groups, clear, 0)
    lax.fori_loop(0, groups, pass_a, 0)
    combine_plane(first_order(jnp.int32(groups - 1), group))

    def weight_tile(g, h):
        t = g * 2 + h
        lse = fin[g, pl.ds(h, 1), :] + jnp.log(fin[g, pl.ds(4 + h, 1), :])
        c = (jnp.exp(logits[t] - lse) - hits(t).astype(jnp.float32)) / softness_divisor
        c = jnp.concatenate([c] * (lanes // 128), axis=1)
        coef[...] = c / sums[t]
        out = jnp.zeros((128, lanes), jnp.float32)
        for b in range(blocks):
            part = pl.ds(b * block_rows, block_rows)
            c = coef[b * (docs // blocks):(b + 1) * (docs // blocks), :].astype(jnp.bfloat16)
            w = jnp.broadcast_to(c[:, None, :], (docs // blocks, length, lanes)).reshape(block_rows, lanes)
            w = powered[t, part, :] * w
            out = out + jnp.dot(doc_t[:, part], w, preferred_element_type=jnp.float32)
        partial[h] = out.T.reshape(tokens, HALF, 128)

    def send_grad(g):
        def body(j, carry):
            peer = peer_of(j)
            to_peer(
                gsend.at[g * tokens + peer], grecv.at[g * tokens + me], send_sem.at[3], g_recv.at[g], peer
            ).start()
            return carry

        lax.fori_loop(1, tokens, body, 0)

    def plane_sum(g):
        wait_in(grecv.at[pl.ds(0, tokens - 1)], g_recv.at[g])
        return jnp.sum(grecv[pl.ds(g * tokens, tokens)].astype(jnp.float32), axis=0)

    def pass_b(k, carry):
        g = last_order(k, group, groups)
        combine_groups(g)

        def tile(h, c):
            weight_tile(g, h)
            return c

        lax.fori_loop(0, 2, tile, 0)
        both = jnp.concatenate([partial[0], partial[1]], axis=1)
        gsend[pl.ds(g * tokens, tokens)] = both.astype(jnp.bfloat16)
        grecv[g * tokens + me] = gsend[g * tokens + me]
        send_grad(g)

        @pl.when(k > 0)
        def _():
            before = last_order(k - 1, group, groups)
            block = yrecv.at[group * groups + before]
            yrecv[group * groups + before] = plane_sum(before)
            to_group(block, yrecv.at[group * groups + before], send_sem.at[4], y_recv, before).start()

        return carry

    lax.fori_loop(0, groups, pass_b, 0)

    loss = jnp.zeros((2, 128), jnp.float32)
    for g in range(groups):
        loss = loss + (fin[g, 0:2, :] + jnp.log(fin[g, 4:6, :]) - fin[g, 6:8, :])
    scale = 1.0 / ((128 // HALF) * groups * ROWS)
    loss_ref[...] = jnp.sum(jnp.sum(loss, axis=0, keepdims=True), axis=1, keepdims=True) * scale

    grad = plane_sum(group)
    if groups > 1:
        wait_in(yrecv.at[pl.ds(0, groups - 1)], y_recv)
        for j in range(1, groups):
            grad = grad + yrecv[other_group(j) * groups + group]
    along = jnp.sum(q_unit * grad, axis=-1, keepdims=True)
    grad_ref[...] = (grad - q_unit * along) / q_length

    many = groups * (tokens - 1)
    wait_out(qbuf.at[pl.ds(0, many + groups - 1)], send_sem.at[0])
    wait_out(st1.at[pl.ds(0, many)], send_sem.at[1])
    wait_out(gsend.at[pl.ds(0, many)], send_sem.at[3])
    if groups > 1:
        wait_out(st2.at[pl.ds(0, groups * (groups - 1))], send_sem.at[2])
        wait_out(yrecv.at[pl.ds(0, groups - 1)], send_sem.at[4])


def on_device(groups, tokens, queries, positive, queue, slot_order):
    docs, length, dim = queue.shape
    rows = docs * length
    lanes = HALF * tokens
    vmem = 63 * 2**20
    VM = pl.BlockSpec(memory_space=pltpu.VMEM)
    chunks = 8 if docs % 8 == 0 else 1
    f32, bf16 = jnp.float32, jnp.bfloat16
    DMA = pltpu.SemaphoreType.DMA
    grad, loss = pl.pallas_call(
        functools.partial(kernel, groups, tokens, docs, length, chunks, vmem),
        out_shape=(jax.ShapeDtypeStruct((ROWS, dim), f32), jax.ShapeDtypeStruct((1, 1), f32)),
        in_specs=[pl.BlockSpec(memory_space=pltpu.SMEM), VM, VM, pl.BlockSpec(memory_space=pl.ANY)],
        out_specs=(VM, VM),
        scratch_shapes=[
            pltpu.VMEM((2 * groups, rows, lanes), bf16),
            pltpu.VMEM((rows, dim), bf16),
            pltpu.VMEM((dim, rows), bf16),
            pltpu.VMEM((groups * tokens, ROWS, dim), bf16),
            pltpu.VMEM((2 * groups, docs, lanes), f32),
            pltpu.VMEM((2 * groups, docs, 128), f32),
            pltpu.VMEM((docs, lanes), f32),
            pltpu.VMEM((docs, 128), f32),
            pltpu.VMEM((groups * tokens, 8, 128), f32),
            pltpu.VMEM((groups * groups, 8, 128), f32),
            pltpu.VMEM((groups, 8, 128), f32),
            pltpu.VMEM((groups * tokens, ROWS, dim), bf16),
            pltpu.VMEM((groups * tokens, ROWS, dim), bf16),
            pltpu.VMEM((groups * groups, ROWS, dim), f32),
            pltpu.VMEM((2, tokens, HALF, dim), f32),
            DMA((chunks,)),
            DMA((groups,)),
            DMA((groups,)),
            DMA((groups,)),
            DMA((groups,)),
            DMA((groups,)),
            DMA,
            DMA((5,)),
        ],
        compiler_params=pltpu.CompilerParams(
            collective_id=0, has_side_effects=True, vmem_limit_bytes=vmem
        ),
    )(positive, queries.reshape(ROWS, dim), slot_order.reshape(1, docs), queue.reshape(rows, dim))
    return loss.reshape(()), grad.reshape(1, ROWS, dim)


def solution(mesh):
    groups, tokens = mesh.shape["group"], mesh.shape["queue"]
    return jax.shard_map(
        functools.partial(on_device, groups, tokens),
        mesh=mesh,
        in_specs=(
            P("queue", "group", None),
            P(),
            P(("group", "queue"), None, None),
            P(("group", "queue")),
        ),
        out_specs=(P(), P("queue", "group", None)),
        check_vma=False,
    )
```

time: 440 us -> 64 us (0.15)
  blocking collectives: 168 us -> 0 us
  waiting for transfers between devices: 144 us -> 0 us
  matrix products: 93.9 us -> 0 us
  Pallas kernels: 0 us -> 60.1 us
  other arithmetic: 13.5 us -> 0 us
  between operations: 15.9 us -> 2.4 us
    psum x1 -> x0, waiting for transfers between devices: 144 us -> none  [on_device(): summed = lax.psum(every_term, ('group', 'queue'))]
    dot_general x48 -> x0, matrix products: 93.9 us -> none  [the longest x32 57.7 us: token_terms(): jnp.einsum('tbk,djk->tbjd', query_block, documents, preferred_element_typ...]
    pmax x1 -> x0, blocking collectives: 66.5 us -> none  [on_device(): top = lax.pmax(local_top, ('group', 'queue'))]
    psum x1 -> x0, blocking collectives: 62.5 us -> none  [on_device(): total, target = lax.psum((local_total, local_target), ('group', 'queue'))]
    pallas_call x0 -> x1, Pallas kernels: none -> 60.1 us  [on_device(): pl.pallas_call(functools.partial(kernel, groups, tokens, docs, length, ch...]
    all_gather x2 -> x0, blocking collectives: 38.8 us -> none  [the longest x1 27.2 us: on_device(): all_tokens = lax.all_gather(query_half, 'queue', axis=0, tiled=True)]
    reduce_sum x21 -> x0, other arithmetic: 6.38 us -> none  [the longest x2 4.38 us: unit_vectors(): length = jnp.sqrt(jnp.sum(wide * wide, axis=-1, keepdims=True) + epsilon)]
    convert_element_type x2 -> x0, other arithmetic: 5.35 us -> none  [the longest x1 4.58 us: on_device(): doc_half = unit_vectors(queue)[0].astype(jnp.bfloat16)]
  transfers between devices with their start and end apart: 1 -> 0, of which waited for: 1 -> 0; matrix products, arithmetic and copies ran while one was open for 0% -> 0% of each run, Pallas kernels for 0% -> 0%
where the time goes in v1:
time: 64 us; the launch traced here: 63.8 us
  Pallas kernels  60.1 us (94%)
  between operations  2.4 us (4%)
  local copies, waits for them, and re-layouts  1.3 us (2%)
    pallas_call x1, Pallas kernels, on_device(): pl.pallas_call(functools.partial(kernel, groups, tokens, docs, length, ch...  60.1 us
    unnamed x1, local copies, waits for them, and re-layouts  1.3 us

profile of v1, /device:TPU:1, one launch (start us, length us, event | category | flops | bytes accessed | tf_op | source)
XLA Modules:
  0.0 63.8 jit_solution(7405214375078810020)
XLA Ops:
  0.6 60.1 %shard_map.59 = (f32[16,128]{1,0:T(8,128)}, f32[1,1]{1,0:T(1,128)}) custom-call(s32[64]{0:T(128)} %pos_ref.1, bf16[16,128]{1,0:T(8,128)(2,1)} %bitcast.7, s32[1,128]{1,0:T(1,128)} %bitcast.8, bf16[12288,128]{1,0:T(8,128)(2,1)} %bitcast.5), custom_call_target="tpu_custom_call" | custom-call | tf_op jit(solution)/shard_map/pallas_call | solution.py:307
  61.4 1.3 %copy.9 = f32[1,16,128]{2,1,0:T(8,128)} copy(f32[1,16,128]{2,1,0:T(8,128)} %bitcast.6) | data formatting | bytes 16384

commit v2 on v1

--- a/solution.py
+++ b/solution.py
@@ -14,6 +14,7 @@
 MESH = pl.DeviceIdType.MESH
 ROWS = 16
 HALF = 8
+SUB = 8
 
 
 def first_order(k, group):
@@ -32,7 +33,7 @@
     groups, tokens, docs, length, chunks, vmem,
     pos_ref, q_ref, slot_ref, queue_ref,
     grad_ref, loss_ref,
-    powered, doc, doc_t, qbuf, sums, logits, coef, slot_col, st1, st2, fin, gsend, grecv, yrecv, partial,
+    powered, doc, doc_t, qbuf, sums, logits, slot_col, st1, st2, fin, gsend, grecv, yrecv,
     load_sem, qy_recv, q_recv, s1_recv, s2_recv, g_recv, y_recv, send_sem,
 ):
     group = lax.axis_index("group")
@@ -40,8 +41,9 @@
     rows = docs * length
     lanes = HALF * tokens
     chunk = rows // chunks
-    blocks = 4
+    blocks = 8
     block_rows = rows // blocks
+    block_docs = docs // blocks
 
     def load(c):
         part = pl.ds(c * chunk, chunk)
@@ -58,11 +60,8 @@
 
     barrier = pltpu.get_barrier_semaphore()
 
-    def greet(j, carry):
+    for j in range(1, tokens):
         pl.semaphore_signal(barrier, inc=1, device_id={"queue": peer_of(j)}, device_id_type=MESH)
-        return carry
-
-    lax.fori_loop(1, tokens, greet, 0)
     for j in range(1, groups):
         pl.semaphore_signal(barrier, inc=1, device_id={"group": other_group(j)}, device_id_type=MESH)
 
@@ -96,14 +95,14 @@
     for j in range(1, groups):
         to_group(mine, mine, send_sem.at[0], qy_recv.at[group], other_group(j)).start()
 
+    def to_all(src_of, dst, send, recv):
+        for j in range(1, tokens):
+            peer = peer_of(j)
+            to_peer(src_of(peer), dst, send, recv, peer).start()
+
     def spread(g):
         block = qbuf.at[g * tokens + me]
-
-        def body(j, carry):
-            to_peer(block, block, send_sem.at[0], q_recv.at[g], peer_of(j)).start()
-            return carry
-
-        lax.fori_loop(1, tokens, body, 0)
+        to_all(lambda peer: block, block, send_sem.at[0], q_recv.at[g])
 
     spread(group)
 
@@ -112,6 +111,7 @@
         part = pl.ds(c * chunk, chunk)
         x = doc[part, :].astype(jnp.float32)
         y = x * lax.rsqrt(jnp.sum(x * x, axis=-1, keepdims=True) + epsilon)
+        y = y.reshape(chunk // (SUB * length), SUB, length, 128).swapaxes(1, 2).reshape(chunk, 128)
         doc[part, :] = y.astype(jnp.bfloat16)
         doc_t[:, part] = y.T.astype(jnp.bfloat16)
 
@@ -128,53 +128,64 @@
                 pass_on(j)
 
     lane = lax.broadcasted_iota(jnp.int32, (1, 128), 1)
-    lane = lax.rem(lane, HALF)
+    spot = lax.rem(lane, HALF)
+    field = lax.div(lane, HALF)
 
     def hits(t):
         wanted = jnp.zeros((1, 128), jnp.float32)
         for b in range(HALF):
-            wanted = jnp.where(lane == b, pos_ref[t * HALF + b].astype(jnp.float32), wanted)
+            wanted = jnp.where(spot == b, pos_ref[t * HALF + b].astype(jnp.float32), wanted)
         return slot_col[...] == wanted
 
-    def score_tile(g, h):
+    def everywhere(x):
+        for shift in (8, 16, 32, 64):
+            x = x + pltpu.roll(x, shift, 1)
+        return x
+
+    def query_tile(g, h):
+        q = qbuf[pl.ds(g * tokens, tokens)].astype(jnp.float32)[:, h * HALF:(h + 1) * HALF]
+        return q.reshape(lanes, 128).T.astype(jnp.bfloat16)
+
+    def dots(g, h):
         t = g * 2 + h
-        q = qbuf[pl.ds(g * tokens, tokens)].astype(jnp.float32)
-        q = jnp.where(h == 0, q[:, :HALF], q[:, HALF:])
-        q = q.reshape(lanes, 128).T.astype(jnp.bfloat16)
+        q = query_tile(g, h)
         for c in range(blocks):
             part = pl.ds(c * block_rows, block_rows)
             x = jnp.dot(doc[part, :], q, preferred_element_type=jnp.float32)
             e = jnp.exp2(x * (log2e / sharpness))
             powered[t, part, :] = e.astype(jnp.bfloat16)
-            summed = jnp.sum(e.reshape(docs // blocks, length, lanes), axis=1)
-            sums[t, c * (docs // blocks):(c + 1) * (docs // blocks), :] = summed
+            summed = jnp.sum(e.reshape(block_docs // SUB, length, SUB, lanes), axis=1)
+            sums[t, c * block_docs:(c + 1) * block_docs, :] = summed.reshape(block_docs, lanes)
+
+    def scores(g, h):
+        t = g * 2 + h
         score = jnp.log(sums[t]) * (sharpness / softness_divisor)
         total = score[:, :128]
         for c in range(1, lanes // 128):
             total = total + score[:, c * 128:(c + 1) * 128]
-        for shift in (8, 16, 32, 64):
-            total = total + pltpu.roll(total, shift, 1)
+        total = everywhere(total)
         logits[t] = total
         top = jnp.max(total, axis=0, keepdims=True)
-        row = g * tokens + me
-        st1[row, pl.ds(h, 1), :] = top
-        st1[row, pl.ds(4 + h, 1), :] = jnp.sum(jnp.exp(total - top), axis=0, keepdims=True)
-        st1[row, pl.ds(6 + h, 1), :] = jnp.sum(jnp.where(hits(t), total, 0.0), axis=0, keepdims=True)
+        mass = jnp.sum(jnp.exp(total - top), axis=0, keepdims=True)
+        target = jnp.sum(jnp.where(hits(t), total, 0.0), axis=0, keepdims=True)
+        row = jnp.where(field == h, top, 0.0)
+        row = jnp.where(field == 4 + h, mass, row)
+        row = jnp.where(field == 6 + h, target, row)
+        at = g * tokens + me
+        if h == 0:
+            st1[at] = row
+        else:
+            st1[at] = st1[at] + row
 
     def combine(parts):
         top = jnp.max(parts, axis=0)
-        scale = jnp.exp(pltpu.roll(parts, 4, 1) - pltpu.roll(top, 4, 0)[None])
-        row = lax.broadcasted_iota(jnp.int32, (8, 128), 0)
-        return jnp.where(row < 4, top, jnp.sum(parts * scale, axis=0))
+        shifted = pltpu.roll(parts.reshape(-1, 128), 32, 1).reshape(parts.shape)
+        scale = jnp.exp(shifted - pltpu.roll(top, 32, 1)[None])
+        return jnp.where(field < 4, top, jnp.sum(parts * scale, axis=0))
 
     def send_stats(g):
         block = st1.at[g * tokens + me]
-
-        def body(j, carry):
-            to_peer(block, block, send_sem.at[1], s1_recv.at[g], peer_of(j)).start()
-            return carry
-
-        lax.fori_loop(1, tokens, body, 0)
+        to_all(lambda peer: block, block, send_sem.at[1], s1_recv.at[g])
 
     def combine_plane(g):
         wait_in(st1.at[pl.ds(0, tokens - 1)], s1_recv.at[g])
@@ -189,59 +200,58 @@
 
     def pass_a(k, carry):
         g = first_order(k, group)
+        before = first_order(k - 1 + lax.div(4 - k, 4), group)
 
         @pl.when(k > 0)
         def _():
             wait_in(qbuf.at[pl.ds(0, tokens - 1)], q_recv.at[g])
 
-        def tile(h, c):
-            score_tile(g, h)
-            return c
-
-        lax.fori_loop(0, 2, tile, 0)
-        send_stats(g)
+        scores(before, 1)
+        dots(g, 0)
 
         @pl.when(k > 0)
         def _():
-            combine_plane(first_order(k - 1, group))
+            send_stats(before)
+
+        scores(g, 0)
+        dots(g, 1)
+
+        @pl.when(k > 0)
+        def _():
+            combine_plane(before)
 
         return carry
 
+    sums[group * 2 + 1] = jnp.ones((docs, lanes), jnp.float32)
+    st1[group * tokens + me] = jnp.zeros((1, 128), jnp.float32)
     wait_in(qbuf.at[pl.ds(0, tokens - 1)], q_recv.at[group])
-    zero = jnp.zeros((2, 128), jnp.float32)
-
-    def clear(g, carry):
-        st1[g * tokens + me, 2:4, :] = zero
-        return carry
-
-    lax.fori_loop(0, groups, clear, 0)
     lax.fori_loop(0, groups, pass_a, 0)
-    combine_plane(first_order(jnp.int32(groups - 1), group))
-
-    def weight_tile(g, h):
+    last = first_order(jnp.int32(groups - 1), group)
+    scores(last, 1)
+    send_stats(last)
+
+    def weight(g, h):
         t = g * 2 + h
-        lse = fin[g, pl.ds(h, 1), :] + jnp.log(fin[g, pl.ds(4 + h, 1), :])
+        row = fin[g]
+        lse = row + jnp.log(pltpu.roll(row, 96, 1))
+        lse = everywhere(jnp.where(field == h, lse, 0.0))
         c = (jnp.exp(logits[t] - lse) - hits(t).astype(jnp.float32)) / softness_divisor
         c = jnp.concatenate([c] * (lanes // 128), axis=1)
-        coef[...] = c / sums[t]
+        return c / sums[t]
+
+    def gradient(g, h, c):
+        t = g * 2 + h
         out = jnp.zeros((128, lanes), jnp.float32)
         for b in range(blocks):
             part = pl.ds(b * block_rows, block_rows)
-            c = coef[b * (docs // blocks):(b + 1) * (docs // blocks), :].astype(jnp.bfloat16)
-            w = jnp.broadcast_to(c[:, None, :], (docs // blocks, length, lanes)).reshape(block_rows, lanes)
-            w = powered[t, part, :] * w
+            w = []
+            for d in range(b * block_docs, (b + 1) * block_docs, SUB):
+                twice = jnp.concatenate([c[d:d + SUB]] * 2, axis=0).astype(jnp.bfloat16)
+                p = powered[t, pl.ds(d * length, SUB * length), :]
+                w.append((p.reshape(length // 2, 2 * SUB, lanes) * twice[None]).reshape(SUB * length, lanes))
+            w = jnp.concatenate(w, axis=0)
             out = out + jnp.dot(doc_t[:, part], w, preferred_element_type=jnp.float32)
-        partial[h] = out.T.reshape(tokens, HALF, 128)
-
-    def send_grad(g):
-        def body(j, carry):
-            peer = peer_of(j)
-            to_peer(
-                gsend.at[g * tokens + peer], grecv.at[g * tokens + me], send_sem.at[3], g_recv.at[g], peer
-            ).start()
-            return carry
-
-        lax.fori_loop(1, tokens, body, 0)
+        return out.T.reshape(tokens, HALF, 128)
 
     def plane_sum(g):
         wait_in(grecv.at[pl.ds(0, tokens - 1)], g_recv.at[g])
@@ -250,33 +260,33 @@
     def pass_b(k, carry):
         g = last_order(k, group, groups)
         combine_groups(g)
-
-        def tile(h, c):
-            weight_tile(g, h)
-            return c
-
-        lax.fori_loop(0, 2, tile, 0)
-        both = jnp.concatenate([partial[0], partial[1]], axis=1)
+        c = [weight(g, h) for h in range(2)]
+        both = jnp.concatenate([gradient(g, h, c[h]) for h in range(2)], axis=1)
         gsend[pl.ds(g * tokens, tokens)] = both.astype(jnp.bfloat16)
         grecv[g * tokens + me] = gsend[g * tokens + me]
-        send_grad(g)
+        to_all(lambda peer: gsend.at[g * tokens + peer], grecv.at[g * tokens + me], send_sem.at[3], g_recv.at[g])
+
+        @pl.when(k == 0)
+        def _():
+            combine_plane(last)
 
         @pl.when(k > 0)
         def _():
             before = last_order(k - 1, group, groups)
             block = yrecv.at[group * groups + before]
             yrecv[group * groups + before] = plane_sum(before)
-            to_group(block, yrecv.at[group * groups + before], send_sem.at[4], y_recv, before).start()
+            to_group(block, block, send_sem.at[4], y_recv, before).start()
 
         return carry
 
     lax.fori_loop(0, groups, pass_b, 0)
 
-    loss = jnp.zeros((2, 128), jnp.float32)
+    loss = jnp.zeros((1, 128), jnp.float32)
     for g in range(groups):
-        loss = loss + (fin[g, 0:2, :] + jnp.log(fin[g, 4:6, :]) - fin[g, 6:8, :])
-    scale = 1.0 / ((128 // HALF) * groups * ROWS)
-    loss_ref[...] = jnp.sum(jnp.sum(loss, axis=0, keepdims=True), axis=1, keepdims=True) * scale
+        row = fin[g]
+        loss = loss + (row + jnp.log(pltpu.roll(row, 96, 1)) - pltpu.roll(row, 80, 1))
+    loss = jnp.sum(jnp.where(field < 2, loss, 0.0), axis=1, keepdims=True)
+    loss_ref[...] = loss * (1.0 / (groups * ROWS))
 
     grad = plane_sum(group)
     if groups > 1:
@@ -316,15 +326,13 @@
             pltpu.VMEM((groups * tokens, ROWS, dim), bf16),
             pltpu.VMEM((2 * groups, docs, lanes), f32),
             pltpu.VMEM((2 * groups, docs, 128), f32),
-            pltpu.VMEM((docs, lanes), f32),
             pltpu.VMEM((docs, 128), f32),
-            pltpu.VMEM((groups * tokens, 8, 128), f32),
-            pltpu.VMEM((groups * groups, 8, 128), f32),
-            pltpu.VMEM((groups, 8, 128), f32),
+            pltpu.VMEM((groups * tokens, 1, 128), f32),
+            pltpu.VMEM((groups * groups, 1, 128), f32),
+            pltpu.VMEM((groups, 1, 128), f32),
             pltpu.VMEM((groups * tokens, ROWS, dim), bf16),
             pltpu.VMEM((groups * tokens, ROWS, dim), bf16),
             pltpu.VMEM((groups * groups, ROWS, dim), f32),
-            pltpu.VMEM((2, tokens, HALF, dim), f32),
             DMA((chunks,)),
             DMA((groups,)),
             DMA((groups,)),

time: 64 us -> 66 us (1.031)
  Pallas kernels: 60.1 us -> 62.1 us
    pallas_call x1, Pallas kernels: 60.1 us -> 62.1 us  [on_device(): pl.pallas_call(functools.partial(kernel, groups, tokens, docs, length, ch...]
where the time goes in v2:
time: 66 us; the launch traced here: 65.8 us
  Pallas kernels  62.1 us (94%)
  between operations  2.4 us (4%)
  local copies, waits for them, and re-layouts  1.3 us (2%)
    pallas_call x1, Pallas kernels, on_device(): pl.pallas_call(functools.partial(kernel, groups, tokens, docs, length, ch...  62.1 us

profile of v2, /device:TPU:1, one launch (start us, length us, event | category | flops | bytes accessed | tf_op | source)
XLA Modules:
  0.0 65.8 jit_solution(9884370713280942851)
XLA Ops:
  0.6 62.1 %shard_map.59 = (f32[16,128]{1,0:T(8,128)}, f32[1,1]{1,0:T(1,128)}) custom-call(s32[64]{0:T(128)} %pos_ref.1, bf16[16,128]{1,0:T(8,128)(2,1)} %bitcast.7, s32[1,128]{1,0:T(1,128)} %bitcast.8, bf16[12288,128]{1,0:T(8,128)(2,1)} %bitcast.5), custom_call_target="tpu_custom_call" | custom-call | tf_op jit(solution)/shard_map/pallas_call | solution.py:317
  63.4 1.3 %copy.9 = f32[1,16,128]{2,1,0:T(8,128)} copy(f32[1,16,128]{2,1,0:T(8,128)} %bitcast.6) | data formatting | bytes 16384

commit v3 on v2

--- a/solution.py
+++ b/solution.py
@@ -17,10 +17,10 @@
 SUB = 8
 
 
-def first_order(k, group):
-    own = lax.div(4 - k, 4)
-    other = (k - 1) + lax.div(k + 3 - group, 4)
-    return own * group + (1 - own) * other
+def tile_order(u, group):
+    own = lax.div(8 - u, 8)
+    other = (u - 1) + lax.div(u + 7 - 2 * group, 8)
+    return own * (2 * group) + (1 - own) * other
 
 
 def last_order(k, group, groups):
@@ -142,13 +142,11 @@
             x = x + pltpu.roll(x, shift, 1)
         return x
 
-    def query_tile(g, h):
-        q = qbuf[pl.ds(g * tokens, tokens)].astype(jnp.float32)[:, h * HALF:(h + 1) * HALF]
-        return q.reshape(lanes, 128).T.astype(jnp.bfloat16)
-
-    def dots(g, h):
-        t = g * 2 + h
-        q = query_tile(g, h)
+    def dots(t):
+        g, h = lax.div(t, 2), lax.rem(t, 2)
+        q = qbuf[pl.ds(g * tokens, tokens)].astype(jnp.float32)
+        q = jnp.where(h == 0, q[:, :HALF], q[:, HALF:])
+        q = q.reshape(lanes, 128).T.astype(jnp.bfloat16)
         for c in range(blocks):
             part = pl.ds(c * block_rows, block_rows)
             x = jnp.dot(doc[part, :], q, preferred_element_type=jnp.float32)
@@ -157,8 +155,8 @@
             summed = jnp.sum(e.reshape(block_docs // SUB, length, SUB, lanes), axis=1)
             sums[t, c * block_docs:(c + 1) * block_docs, :] = summed.reshape(block_docs, lanes)
 
-    def scores(g, h):
-        t = g * 2 + h
+    def scores(t, valid):
+        g, h = lax.div(t, 2), lax.rem(t, 2)
         score = jnp.log(sums[t]) * (sharpness / softness_divisor)
         total = score[:, :128]
         for c in range(1, lanes // 128):
@@ -171,11 +169,8 @@
         row = jnp.where(field == h, top, 0.0)
         row = jnp.where(field == 4 + h, mass, row)
         row = jnp.where(field == 6 + h, target, row)
-        at = g * tokens + me
-        if h == 0:
-            st1[at] = row
-        else:
-            st1[at] = st1[at] + row
+        at = (valid * g + (1 - valid) * (groups - 1)) * tokens + me
+        st1[at] = st1[at] + jnp.where(valid > 0, row, 0.0)
 
     def combine(parts):
         top = jnp.max(parts, axis=0)
@@ -198,37 +193,37 @@
         wait_in(st2.at[pl.ds(0, groups - 1)], s2_recv.at[g])
         fin[g] = combine(st2[pl.ds(g * groups, groups)])
 
-    def pass_a(k, carry):
-        g = first_order(k, group)
-        before = first_order(k - 1 + lax.div(4 - k, 4), group)
-
-        @pl.when(k > 0)
-        def _():
-            wait_in(qbuf.at[pl.ds(0, tokens - 1)], q_recv.at[g])
-
-        scores(before, 1)
-        dots(g, 0)
-
-        @pl.when(k > 0)
-        def _():
-            send_stats(before)
-
-        scores(g, 0)
-        dots(g, 1)
-
-        @pl.when(k > 0)
-        def _():
-            combine_plane(before)
+    def pass_a(u, carry):
+        t = tile_order(u, group)
+        before = tile_order(u - 1 + lax.div(8 - u, 8), group)
+
+        @pl.when((u > 0) & (lax.rem(t, 2) == 0))
+        def _():
+            wait_in(qbuf.at[pl.ds(0, tokens - 1)], q_recv.at[lax.div(t, 2)])
+
+        scores(before, lax.div(u + last, last + 1) * (1 - lax.div(u, last)))
+        dots(t)
+
+        @pl.when(u >= last - 1)
+        def _():
+            scores(t, 1)
+
+        @pl.when((u >= 3) & (u != 4))
+        def _():
+            send_stats(lax.div(u - 2 + lax.div(u, last), 2))
+
+        @pl.when(u == last - 1)
+        def _():
+            combine_plane(jnp.int32(0))
 
         return carry
 
-    sums[group * 2 + 1] = jnp.ones((docs, lanes), jnp.float32)
-    st1[group * tokens + me] = jnp.zeros((1, 128), jnp.float32)
+    last = 2 * groups - 1
+    sums[group * 2] = jnp.ones((docs, lanes), jnp.float32)
+    for g in range(groups):
+        st1[g * tokens + me] = jnp.zeros((1, 128), jnp.float32)
     wait_in(qbuf.at[pl.ds(0, tokens - 1)], q_recv.at[group])
-    lax.fori_loop(0, groups, pass_a, 0)
-    last = first_order(jnp.int32(groups - 1), group)
-    scores(last, 1)
-    send_stats(last)
+    lax.fori_loop(0, last + 1, pass_a, 0)
 
     def weight(g, h):
         t = g * 2 + h
@@ -259,6 +254,16 @@
 
     def pass_b(k, carry):
         g = last_order(k, group, groups)
+
+        @pl.when(k == 0)
+        def _():
+            combine_plane(jnp.int32(1))
+
+        @pl.when(k == 1 - lax.div(groups - group, groups))
+        def _():
+            combine_plane(jnp.int32(2))
+            combine_plane(jnp.int32(3))
+
         combine_groups(g)
         c = [weight(g, h) for h in range(2)]
         both = jnp.concatenate([gradient(g, h, c[h]) for h in range(2)], axis=1)
@@ -266,20 +271,18 @@
         grecv[g * tokens + me] = gsend[g * tokens + me]
         to_all(lambda peer: gsend.at[g * tokens + peer], grecv.at[g * tokens + me], send_sem.at[3], g_recv.at[g])
 
-        @pl.when(k == 0)
-        def _():
-            combine_plane(last)
-
-        @pl.when(k > 0)
-        def _():
-            before = last_order(k - 1, group, groups)
-            block = yrecv.at[group * groups + before]
-            yrecv[group * groups + before] = plane_sum(before)
-            to_group(block, block, send_sem.at[4], y_recv, before).start()
-
         return carry
 
     lax.fori_loop(0, groups, pass_b, 0)
+
+    def hand_over(k, carry):
+        g = last_order(k, group, groups)
+        block = yrecv.at[group * groups + g]
+        yrecv[group * groups + g] = plane_sum(g)
+        to_group(block, block, send_sem.at[4], y_recv, g).start()
+        return carry
+
+    lax.fori_loop(0, groups - 1, hand_over, 0)
 
     loss = jnp.zeros((1, 128), jnp.float32)
     for g in range(groups):

time: 66 us -> 58.9 us (0.89)
  Pallas kernels: 62.1 us -> 55 us
    pallas_call x1, Pallas kernels: 62.1 us -> 55 us  [on_device(): pl.pallas_call(functools.partial(kernel, groups, tokens, docs, length, ch...]
where the time goes in v3:
time: 58.9 us; the launch traced here: 58.7 us
  Pallas kernels  55 us (93%)
  between operations  2.4 us (4%)
  local copies, waits for them, and re-layouts  1.3 us (2%)
    pallas_call x1, Pallas kernels, on_device(): pl.pallas_call(functools.partial(kernel, groups, tokens, docs, length, ch...  55 us
    unnamed x1, local copies, waits for them, and re-layouts  1.3 us

profile of v3, /device:TPU:1, one launch (start us, length us, event | category | flops | bytes accessed | tf_op | source)
XLA Modules:
  0.0 58.7 jit_solution(5783642084681882861)
XLA Ops:
  0.6 55.0 %shard_map.59 = (f32[16,128]{1,0:T(8,128)}, f32[1,1]{1,0:T(1,128)}) custom-call(s32[64]{0:T(128)} %pos_ref.1, bf16[16,128]{1,0:T(8,128)(2,1)} %bitcast.7, s32[1,128]{1,0:T(1,128)} %bitcast.8, bf16[12288,128]{1,0:T(8,128)(2,1)} %bitcast.5), custom_call_target="tpu_custom_call" | custom-call | tf_op jit(solution)/shard_map/pallas_call | solution.py:320
  56.2 1.3 %copy.9 = f32[1,16,128]{2,1,0:T(8,128)} copy(f32[1,16,128]{2,1,0:T(8,128)} %bitcast.6) | data formatting | bytes 16384

commit v4 on v3

v4 whole, which is shorter than its diff:
```python
import functools

import jax
import jax.numpy as jnp
from jax import lax
from jax.experimental import pallas as pl
from jax.experimental.pallas import tpu as pltpu
from jax.sharding import PartitionSpec as P

sharpness = 0.1
softness_divisor = 0.05
epsilon = 1e-06
log2e = 1.4426950408889634
MESH = pl.DeviceIdType.MESH
ROWS = 16
SUB = 8


def tile_order(u, first):
    own = lax.div(8 - u, 8)
    other = (u - 1) + lax.div(u + 7 - first, 8)
    return own * first + (1 - own) * other


def last_order(k, group, groups):
    own = lax.div(k, groups - 1)
    other = k + lax.div(k - group + 4, 4)
    return own * group + (1 - own) * other


def kernel(
    groups, tokens, docs, length, chunks, vmem,
    pos_ref, q_ref, slot_ref, queue_ref,
    grad_ref, loss_ref,
    powered, doc, doc_t, qbuf, sums, logits, slot_col, stats, fin, gsend, grecv, yrecv,
    load_sem, qy_recv, q_recv, s_recv, g_recv, y_recv, send_sem,
):
    group = lax.axis_index("group")
    me = lax.axis_index("queue")
    rows = docs * length
    half = tokens // 2
    lanes = half * ROWS
    chunk = rows // chunks
    blocks = 8
    block_rows = rows // blocks
    block_docs = docs // blocks
    everyone = groups * tokens

    def load(c):
        part = pl.ds(c * chunk, chunk)
        return pltpu.make_async_copy(queue_ref.at[part], doc.at[part], load_sem.at[c])

    for c in range(chunks):
        load(c).start()

    def peer_of(j):
        return lax.rem(me + j, tokens)

    def other_group(j):
        return lax.rem(group + j, groups)

    barrier = pltpu.get_barrier_semaphore()

    for j in range(1, tokens):
        pl.semaphore_signal(barrier, inc=1, device_id={"queue": peer_of(j)}, device_id_type=MESH)
    for j in range(1, groups):
        pl.semaphore_signal(barrier, inc=1, device_id={"group": other_group(j)}, device_id_type=MESH)

    wide = q_ref[...].astype(jnp.float32)
    q_length = jnp.sqrt(jnp.sum(wide * wide, axis=-1, keepdims=True) + epsilon)
    q_unit = wide / q_length
    qbuf[group * tokens + me] = q_unit.astype(jnp.bfloat16)
    slot_col[...] = jnp.broadcast_to(slot_ref[...].astype(jnp.float32), (128, docs)).T

    pl.semaphore_wait(barrier, tokens - 1 + groups - 1)

    def to_group(src, dst, send, recv, j):
        return pltpu.make_async_remote_copy(
            src_ref=src, dst_ref=dst, send_sem=send, recv_sem=recv,
            device_id={"group": j}, device_id_type=MESH,
        )

    def to_peer(src, dst, send, recv, j):
        return pltpu.make_async_remote_copy(
            src_ref=src, dst_ref=dst, send_sem=send, recv_sem=recv,
            device_id={"queue": j}, device_id_type=MESH,
        )

    def wait_in(ref, sem):
        to_peer(ref, ref, send_sem.at[0], sem, me).wait_recv()

    def wait_out(ref, sem):
        to_peer(ref, ref, sem, q_recv.at[0], me).wait_send()

    mine = qbuf.at[group * tokens + me]
    for j in range(1, groups):
        to_group(mine, mine, send_sem.at[0], qy_recv.at[group], other_group(j)).start()

    mine_half = lax.div(me, half)
    near = [mine_half * half + lax.rem(me - mine_half * half + j, half) for j in range(1, half)]
    far = [(1 - mine_half) * half + j for j in range(half)]

    def spread(g):
        block = qbuf.at[g * tokens + me]
        for peer in near + far:
            to_peer(block, block, send_sem.at[0], q_recv.at[2 * g + mine_half], peer).start()

    spread(group)

    def normalize(c):
        load(c).wait()
        part = pl.ds(c * chunk, chunk)
        x = doc[part, :].astype(jnp.float32)
        y = x * lax.rsqrt(jnp.sum(x * x, axis=-1, keepdims=True) + epsilon)
        y = y.reshape(chunk // (SUB * length), SUB, length, 128).swapaxes(1, 2).reshape(chunk, 128)
        doc[part, :] = y.astype(jnp.bfloat16)
        doc_t[:, part] = y.T.astype(jnp.bfloat16)

    for c in range(chunks):
        normalize(c)

    for k in range(groups - 1):
        g = last_order(k, group, groups)
        wait_in(qbuf.at[g * tokens + me], qy_recv.at[g])
        spread(g)

    lane = lax.broadcasted_iota(jnp.int32, (1, 128), 1)
    spot = lax.rem(lane, ROWS)
    field = lax.div(lane, ROWS)

    def hits(g):
        wanted = jnp.zeros((1, 128), jnp.float32)
        for b in range(ROWS):
            wanted = jnp.where(spot == b, pos_ref[g * ROWS + b].astype(jnp.float32), wanted)
        return slot_col[...] == wanted

    def everywhere(x):
        for shift in (16, 32, 64):
            x = x + pltpu.roll(x, shift, 1)
        return x

    def dots(t):
        q = qbuf[pl.ds(t * half, half)].reshape(lanes, 128).T
        for c in range(blocks):
            part = pl.ds(c * block_rows, block_rows)
            x = jnp.dot(doc[part, :], q, preferred_element_type=jnp.float32)
            e = jnp.exp2(x * (log2e / sharpness))
            powered[t, part, :] = e.astype(jnp.bfloat16)
            summed = jnp.sum(e.reshape(block_docs // SUB, length, SUB, lanes), axis=1)
            sums[t, c * block_docs:(c + 1) * block_docs, :] = summed.reshape(block_docs, lanes)

    def scores(g):
        total = jnp.zeros((docs, 128), jnp.float32)
        for h in range(2):
            score = jnp.log(sums[2 * g + h])
            for c in range(lanes // 128):
                total = total + score[:, c * 128:(c + 1) * 128]
        total = everywhere(total) * (sharpness / softness_divisor)
        logits[g] = total
        top = jnp.max(total, axis=0, keepdims=True)
        mass = jnp.sum(jnp.exp(total - top), axis=0, keepdims=True)
        target = jnp.sum(jnp.where(hits(g), total, 0.0), axis=0, keepdims=True)
        row = jnp.where(field == 0, top, 0.0)
        row = jnp.where(field == 4, mass, row)
        stats[g * everyone + group * tokens + me] = jnp.where(field == 5, target, row)

    def send_stats(g):
        block = stats.at[g * everyone + group * tokens + me]
        for i in range(groups):
            for j in range(tokens):
                if i + j > 0:
                    pltpu.make_async_remote_copy(
                        src_ref=block, dst_ref=block, send_sem=send_sem.at[1], recv_sem=s_recv.at[g],
                        device_id=(other_group(i), peer_of(j)), device_id_type=MESH,
                    ).start()

    def combine(g):
        wait_in(stats.at[pl.ds(0, everyone - 1)], s_recv.at[g])
        parts = stats[pl.ds(g * everyone, everyone)].reshape(everyone, 128)
        top = jnp.max(parts, axis=0, keepdims=True)
        scale = jnp.exp(pltpu.roll(parts, 64, 1) - pltpu.roll(top, 64, 1))
        fin[g] = jnp.where(field < 4, top, jnp.sum(parts * scale, axis=0, keepdims=True))

    def pass_a(u, carry):
        t = tile_order(u, first)

        @pl.when((u > 0) & (lax.rem(t, 2) == mine_half))
        def _():
            wait_in(qbuf.at[pl.ds(0, half - 1)], q_recv.at[t])

        @pl.when((u > 0) & (lax.rem(t, 2) != mine_half))
        def _():
            wait_in(qbuf.at[pl.ds(0, half)], q_recv.at[t])

        dots(t)
        g = lax.div(u + 1, 2) - 1
        odd = lax.rem(u, 2)

        @pl.when(((odd == 1) & (g >= group)) | ((odd == 0) & (u > 0) & (g < group)))
        def _():
            scores(g)
            send_stats(g)

        return carry

    first = 2 * group + mine_half
    wait_in(qbuf.at[pl.ds(0, half - 1)], q_recv.at[first])
    lax.fori_loop(0, 2 * groups, pass_a, 0)

    def gradient(t, c):
        c = jnp.concatenate([c] * (lanes // 128), axis=1) / sums[t]
        out = jnp.zeros((128, lanes), jnp.float32)
        for b in range(blocks):
            part = pl.ds(b * block_rows, block_rows)
            w = []
            for d in range(b * block_docs, (b + 1) * block_docs, SUB):
                twice = jnp.concatenate([c[d:d + SUB]] * 2, axis=0).astype(jnp.bfloat16)
                p = powered[t, pl.ds(d * length, SUB * length), :]
                w.append((p.reshape(length // 2, 2 * SUB, lanes) * twice[None]).reshape(SUB * length, lanes))
            w = jnp.concatenate(w, axis=0)
            out = out + jnp.dot(doc_t[:, part], w, preferred_element_type=jnp.float32)
        gsend[pl.ds(t * half, half)] = out.T.reshape(half, ROWS, 128).astype(jnp.bfloat16)

    def send_grad(g, peers):
        for peer in peers:
            to_peer(
                gsend.at[g * tokens + peer], grecv.at[g * tokens + me], send_sem.at[3], g_recv.at[g], peer
            ).start()

    def plane_sum(g):
        wait_in(grecv.at[pl.ds(0, tokens - 1)], g_recv.at[g])
        return jnp.sum(grecv[pl.ds(g * tokens, tokens)].astype(jnp.float32), axis=0)

    def pass_b(k, carry):
        g = last_order(k, group, groups)

        combine(g)
        row = fin[g]
        lse = everywhere(jnp.where(field == 0, row + jnp.log(pltpu.roll(row, 64, 1)), 0.0))
        c = (jnp.exp(logits[g] - lse) - hits(g).astype(jnp.float32)) / softness_divisor
        gradient(2 * g + 1 - mine_half, c)
        send_grad(g, far)
        gradient(2 * g + mine_half, c)
        grecv[g * tokens + me] = gsend[g * tokens + me]
        send_grad(g, near)
        return carry

    lax.fori_loop(0, groups, pass_b, 0)

    def hand_over(k, carry):
        g = last_order(k, group, groups)
        block = yrecv.at[group * groups + g]
        yrecv[group * groups + g] = plane_sum(g)
        to_group(block, block, send_sem.at[4], y_recv, g).start()
        return carry

    lax.fori_loop(0, groups - 1, hand_over, 0)

    loss = jnp.zeros((1, 128), jnp.float32)
    for g in range(groups):
        row = fin[g]
        loss = loss + (row + jnp.log(pltpu.roll(row, 64, 1)) - pltpu.roll(row, 48, 1))
    loss = jnp.sum(jnp.where(field == 0, loss, 0.0), axis=1, keepdims=True)
    loss_ref[...] = loss * (1.0 / (groups * ROWS))

    grad = plane_sum(group)
    if groups > 1:
        wait_in(yrecv.at[pl.ds(0, groups - 1)], y_recv)
        for j in range(1, groups):
            grad = grad + yrecv[other_group(j) * groups + group]
    along = jnp.sum(q_unit * grad, axis=-1, keepdims=True)
    grad_ref[...] = (grad - q_unit * along) / q_length

    many = groups * (tokens - 1)
    wait_out(qbuf.at[pl.ds(0, many + groups - 1)], send_sem.at[0])
    wait_out(stats.at[pl.ds(0, groups * (everyone - 1))], send_sem.at[1])
    wait_out(gsend.at[pl.ds(0, many)], send_sem.at[3])
    if groups > 1:
        wait_out(yrecv.at[pl.ds(0, groups - 1)], send_sem.at[4])


def on_device(groups, tokens, queries, positive, queue, slot_order):
    docs, length, dim = queue.shape
    rows = docs * length
    half = tokens // 2
    lanes = half * ROWS
    vmem = 63 * 2**20
    VM = pl.BlockSpec(memory_space=pltpu.VMEM)
    chunks = 8 if docs % 8 == 0 else 1
    f32, bf16 = jnp.float32, jnp.bfloat16
    DMA = pltpu.SemaphoreType.DMA
    grad, loss = pl.pallas_call(
        functools.partial(kernel, groups, tokens, docs, length, chunks, vmem),
        out_shape=(jax.ShapeDtypeStruct((ROWS, dim), f32), jax.ShapeDtypeStruct((1, 1), f32)),
        in_specs=[pl.BlockSpec(memory_space=pltpu.SMEM), VM, VM, pl.BlockSpec(memory_space=pl.ANY)],
        out_specs=(VM, VM),
        scratch_shapes=[
            pltpu.VMEM((2 * groups, rows, lanes), bf16),
            pltpu.VMEM((rows, dim), bf16),
            pltpu.VMEM((dim, rows), bf16),
            pltpu.VMEM((groups * tokens, ROWS, dim), bf16),
            pltpu.VMEM((2 * groups, docs, lanes), f32),
            pltpu.VMEM((groups, docs, 128), f32),
            pltpu.VMEM((docs, 128), f32),
            pltpu.VMEM((groups * groups * tokens, 1, 128), f32),
            pltpu.VMEM((groups, 1, 128), f32),
            pltpu.VMEM((groups * tokens, ROWS, dim), bf16),
            pltpu.VMEM((groups * tokens, ROWS, dim), bf16),
            pltpu.VMEM((groups * groups, ROWS, dim), f32),
            DMA((chunks,)),
            DMA((groups,)),
            DMA((2 * groups,)),
            DMA((groups,)),
            DMA((groups,)),
            DMA,
            DMA((5,)),
        ],
        compiler_params=pltpu.CompilerParams(
            collective_id=0, has_side_effects=True, vmem_limit_bytes=vmem
        ),
    )(positive, queries.reshape(ROWS, dim), slot_order.reshape(1, docs), queue.reshape(rows, dim))
    return loss.reshape(()), grad.reshape(1, ROWS, dim)


def solution(mesh):
    groups, tokens = mesh.shape["group"], mesh.shape["queue"]
    return jax.shard_map(
        functools.partial(on_device, groups, tokens),
        mesh=mesh,
        in_specs=(
            P("queue", "group", None),
            P(),
            P(("group", "queue"), None, None),
            P(("group", "queue")),
        ),
        out_specs=(P(), P("queue", "group", None)),
        check_vma=False,
    )
```

time: 58.9 us -> 59.7 us (1.014)
  Pallas kernels: 55 us -> 55.8 us
    pallas_call x1, Pallas kernels: 55 us -> 55.8 us  [on_device(): pl.pallas_call(functools.partial(kernel, groups, tokens, docs, length, ch...]
where the time goes in v4:
time: 59.7 us; the launch traced here: 59.5 us
  Pallas kernels  55.8 us (93%)
  between operations  2.4 us (4%)
  local copies, waits for them, and re-layouts  1.3 us (2%)
    pallas_call x1, Pallas kernels, on_device(): pl.pallas_call(functools.partial(kernel, groups, tokens, docs, length, ch...  55.8 us
    unnamed x1, local copies, waits for them, and re-layouts  1.3 us

profile of v4, /device:TPU:1, one launch (start us, length us, event | category | flops | bytes accessed | tf_op | source)
XLA Modules:
  0.0 59.5 jit_solution(5792511229885828057)
XLA Ops:
  0.6 55.8 %shard_map.59 = (f32[16,128]{1,0:T(8,128)}, f32[1,1]{1,0:T(1,128)}) custom-call(s32[64]{0:T(128)} %pos_ref.1, bf16[16,128]{1,0:T(8,128)(2,1)} %bitcast.7, s32[1,128]{1,0:T(1,128)} %bitcast.8, bf16[12288,128]{1,0:T(8,128)(2,1)} %bitcast.5), custom_call_target="tpu_custom_call" | custom-call | tf_op jit(solution)/shard_map/pallas_call | solution.py:292
  57.1 1.3 %copy.9 = f32[1,16,128]{2,1,0:T(8,128)} copy(f32[1,16,128]{2,1,0:T(8,128)} %bitcast.6) | data formatting | bytes 16384

commit v5 on v4

--- a/solution.py
+++ b/solution.py
@@ -98,7 +98,7 @@
 
     mine_half = lax.div(me, half)
     near = [mine_half * half + lax.rem(me - mine_half * half + j, half) for j in range(1, half)]
-    far = [(1 - mine_half) * half + j for j in range(half)]
+    far = [(1 - mine_half) * half + lax.rem(me - mine_half * half + j, half) for j in range(half)]
 
     def spread(g):
         block = qbuf.at[g * tokens + me]
@@ -239,10 +239,9 @@
         lse = everywhere(jnp.where(field == 0, row + jnp.log(pltpu.roll(row, 64, 1)), 0.0))
         c = (jnp.exp(logits[g] - lse) - hits(g).astype(jnp.float32)) / softness_divisor
         gradient(2 * g + 1 - mine_half, c)
-        send_grad(g, far)
         gradient(2 * g + mine_half, c)
         grecv[g * tokens + me] = gsend[g * tokens + me]
-        send_grad(g, near)
+        send_grad(g, near + far)
         return carry
 
     lax.fori_loop(0, groups, pass_b, 0)

time: 59.7 us -> 56.1 us (0.940)
  Pallas kernels: 55.8 us -> 52.2 us
    pallas_call x1, Pallas kernels: 55.8 us -> 52.2 us  [on_device(): pl.pallas_call(functools.partial(kernel, groups, tokens, docs, length, ch...]
where the time goes in v5:
time: 56.1 us; the launch traced here: 55.9 us
  Pallas kernels  52.2 us (93%)
  between operations  2.4 us (4%)
  local copies, waits for them, and re-layouts  1.3 us (2%)
    pallas_call x1, Pallas kernels, on_device(): pl.pallas_call(functools.partial(kernel, groups, tokens, docs, length, ch...  52.2 us
    unnamed x1, local copies, waits for them, and re-layouts  1.3 us

profile of v5, /device:TPU:1, one launch (start us, length us, event | category | flops | bytes accessed | tf_op | source)
XLA Modules:
  0.0 55.9 jit_solution(17105152751402671106)
XLA Ops:
  0.6 52.2 %shard_map.59 = (f32[16,128]{1,0:T(8,128)}, f32[1,1]{1,0:T(1,128)}) custom-call(s32[64]{0:T(128)} %pos_ref.1, bf16[16,128]{1,0:T(8,128)(2,1)} %bitcast.7, s32[1,128]{1,0:T(1,128)} %bitcast.8, bf16[12288,128]{1,0:T(8,128)(2,1)} %bitcast.5), custom_call_target="tpu_custom_call" | custom-call | tf_op jit(solution)/shard_map/pallas_call | solution.py:291
  53.5 1.3 %copy.9 = f32[1,16,128]{2,1,0:T(8,128)} copy(f32[1,16,128]{2,1,0:T(8,128)} %bitcast.6) | data formatting | bytes 16384

commit v6 on v5

--- a/solution.py
+++ b/solution.py
@@ -16,10 +16,10 @@
 SUB = 8
 
 
-def tile_order(u, first):
-    own = lax.div(8 - u, 8)
-    other = (u - 1) + lax.div(u + 7 - first, 8)
-    return own * first + (1 - own) * other
+def first_order(k, group):
+    own = lax.div(4 - k, 4)
+    other = (k - 1) + lax.div(k + 3 - group, 4)
+    return own * group + (1 - own) * other
 
 
 def last_order(k, group, groups):
@@ -181,31 +181,42 @@
         scale = jnp.exp(pltpu.roll(parts, 64, 1) - pltpu.roll(top, 64, 1))
         fin[g] = jnp.where(field < 4, top, jnp.sum(parts * scale, axis=0, keepdims=True))
 
-    def pass_a(u, carry):
-        t = tile_order(u, first)
-
-        @pl.when((u > 0) & (lax.rem(t, 2) == mine_half))
+    def wait_near(t):
+        wait_in(qbuf.at[pl.ds(0, half - 1)], q_recv.at[t])
+
+    def wait_far(t):
+        wait_in(qbuf.at[pl.ds(0, half)], q_recv.at[t])
+
+    def own_tile(i, carry):
+        t = 2 * group + lax.rem(mine_half + i, 2)
+
+        @pl.when(i == 0)
         def _():
-            wait_in(qbuf.at[pl.ds(0, half - 1)], q_recv.at[t])
-
-        @pl.when((u > 0) & (lax.rem(t, 2) != mine_half))
+            wait_near(t)
+
+        @pl.when(i == 1)
         def _():
-            wait_in(qbuf.at[pl.ds(0, half)], q_recv.at[t])
+            wait_far(t)
 
         dots(t)
-        g = lax.div(u + 1, 2) - 1
-        odd = lax.rem(u, 2)
-
-        @pl.when(((odd == 1) & (g >= group)) | ((odd == 0) & (u > 0) & (g < group)))
-        def _():
-            scores(g)
-            send_stats(g)
-
         return carry
 
-    first = 2 * group + mine_half
-    wait_in(qbuf.at[pl.ds(0, half - 1)], q_recv.at[first])
-    lax.fori_loop(0, 2 * groups, pass_a, 0)
+    def pass_a(k, carry):
+        g = first_order(k, group)
+        before = first_order(k - 1, group)
+        wait_near(2 * g + mine_half)
+        wait_far(2 * g + 1 - mine_half)
+        scores(before)
+        send_stats(before)
+        dots(2 * g)
+        dots(2 * g + 1)
+        return carry
+
+    lax.fori_loop(0, 2, own_tile, 0)
+    lax.fori_loop(1, groups, pass_a, 0)
+    final = first_order(jnp.int32(groups - 1), group)
+    scores(final)
+    send_stats(final)
 
     def gradient(t, c):
         c = jnp.concatenate([c] * (lanes // 128), axis=1) / sums[t]
@@ -231,8 +242,11 @@
         wait_in(grecv.at[pl.ds(0, tokens - 1)], g_recv.at[g])
         return jnp.sum(grecv[pl.ds(g * tokens, tokens)].astype(jnp.float32), axis=0)
 
+    rest = groups - 1 - group
+    pivot = group + rest * lax.div(rest, 2)
+
     def pass_b(k, carry):
-        g = last_order(k, group, groups)
+        g = last_order(k, pivot, groups)
 
         combine(g)
         row = fin[g]

time: 56.1 us -> 54.7 us (0.975)
  Pallas kernels: 52.2 us -> 50.3 us
    pallas_call x1, Pallas kernels: 52.2 us -> 50.3 us  [on_device(): pl.pallas_call(functools.partial(kernel, groups, tokens, docs, length, ch...]
where the time goes in v6:
time: 54.7 us; the launch traced here: 54 us
  Pallas kernels  50.3 us (92%)
  between operations  2.4 us (4%)
  local copies, waits for them, and re-layouts  1.3 us (2%)
    pallas_call x1, Pallas kernels, on_device(): pl.pallas_call(functools.partial(kernel, groups, tokens, docs, length, ch...  50.3 us
    unnamed x1, local copies, waits for them, and re-layouts  1.3 us

profile of v6, /device:TPU:1, one launch (start us, length us, event | category | flops | bytes accessed | tf_op | source)
XLA Modules:
  0.0 54.0 jit_solution(7342987905609296105)
XLA Ops:
  0.6 50.3 %shard_map.59 = (f32[16,128]{1,0:T(8,128)}, f32[1,1]{1,0:T(1,128)}) custom-call(s32[64]{0:T(128)} %pos_ref.1, bf16[16,128]{1,0:T(8,128)(2,1)} %bitcast.7, s32[1,128]{1,0:T(1,128)} %bitcast.8, bf16[12288,128]{1,0:T(8,128)(2,1)} %bitcast.5), custom_call_target="tpu_custom_call" | custom-call | tf_op jit(solution)/shard_map/pallas_call | solution.py:305
  51.5 1.3 %copy.9 = f32[1,16,128]{2,1,0:T(8,128)} copy(f32[1,16,128]{2,1,0:T(8,128)} %bitcast.6) | data formatting | bytes 16384

commit v7 on v6

--- a/solution.py
+++ b/solution.py
@@ -30,10 +30,10 @@
 
 def kernel(
     groups, tokens, docs, length, chunks, vmem,
-    pos_ref, q_ref, slot_ref, queue_ref,
+    pos_in, q_in, slot_in, queue_ref,
     grad_ref, loss_ref,
-    powered, doc, doc_t, qbuf, sums, logits, slot_col, stats, fin, gsend, grecv, yrecv,
-    load_sem, qy_recv, q_recv, s_recv, g_recv, y_recv, send_sem,
+    pos_ref, q_ref, slot_ref, powered, doc, doc_t, qbuf, sums, logits, slot_col, stats, fin, gsend, grecv, yrecv,
+    small_sem, load_sem, qy_recv, q_recv, s_recv, g_recv, y_recv, send_sem,
 ):
     group = lax.axis_index("group")
     me = lax.axis_index("queue")
@@ -50,8 +50,12 @@
         part = pl.ds(c * chunk, chunk)
         return pltpu.make_async_copy(queue_ref.at[part], doc.at[part], load_sem.at[c])
 
-    for c in range(chunks):
-        load(c).start()
+    small = [
+        pltpu.make_async_copy(src, dst, small_sem.at[n])
+        for n, (src, dst) in enumerate(((q_in, q_ref), (slot_in, slot_ref), (pos_in, pos_ref)))
+    ]
+    for copy in small:
+        copy.start()
 
     def peer_of(j):
         return lax.rem(me + j, tokens)
@@ -61,10 +65,19 @@
 
     barrier = pltpu.get_barrier_semaphore()
 
-    for j in range(1, tokens):
+    def hops(j):
+        x, z = j % 8 // 2, j // 8 % 4
+        return min(x, 4 - x) + min(z, 4 - z)
+
+    around = sorted(range(1, tokens), key=hops, reverse=True)
+    for j in around:
         pl.semaphore_signal(barrier, inc=1, device_id={"queue": peer_of(j)}, device_id_type=MESH)
     for j in range(1, groups):
         pl.semaphore_signal(barrier, inc=1, device_id={"group": other_group(j)}, device_id_type=MESH)
+    for c in range(chunks):
+        load(c).start()
+    for copy in small:
+        copy.wait()
 
     wide = q_ref[...].astype(jnp.float32)
     q_length = jnp.sqrt(jnp.sum(wide * wide, axis=-1, keepdims=True) + epsilon)
@@ -97,7 +110,7 @@
         to_group(mine, mine, send_sem.at[0], qy_recv.at[group], other_group(j)).start()
 
     mine_half = lax.div(me, half)
-    near = [mine_half * half + lax.rem(me - mine_half * half + j, half) for j in range(1, half)]
+    near = [mine_half * half + lax.rem(me - mine_half * half + j, half) for j in sorted(range(1, half), key=hops, reverse=True)]
     far = [(1 - mine_half) * half + lax.rem(me - mine_half * half + j, half) for j in range(half)]
 
     def spread(g):
@@ -166,13 +179,12 @@
 
     def send_stats(g):
         block = stats.at[g * everyone + group * tokens + me]
-        for i in range(groups):
-            for j in range(tokens):
-                if i + j > 0:
-                    pltpu.make_async_remote_copy(
-                        src_ref=block, dst_ref=block, send_sem=send_sem.at[1], recv_sem=s_recv.at[g],
-                        device_id=(other_group(i), peer_of(j)), device_id_type=MESH,
-                    ).start()
+        steps = [(i, j) for i in range(groups) for j in range(tokens) if i + j > 0]
+        for i, j in sorted(steps, key=lambda s: hops(s[1]) + min(s[0], groups - s[0]), reverse=True):
+            pltpu.make_async_remote_copy(
+                src_ref=block, dst_ref=block, send_sem=send_sem.at[1], recv_sem=s_recv.at[g],
+                device_id=(other_group(i), peer_of(j)), device_id_type=MESH,
+            ).start()
 
     def combine(g):
         wait_in(stats.at[pl.ds(0, everyone - 1)], s_recv.at[g])
@@ -255,7 +267,7 @@
         gradient(2 * g + 1 - mine_half, c)
         gradient(2 * g + mine_half, c)
         grecv[g * tokens + me] = gsend[g * tokens + me]
-        send_grad(g, near + far)
+        send_grad(g, far + near)
         return carry
 
     lax.fori_loop(0, groups, pass_b, 0)
@@ -305,9 +317,12 @@
     grad, loss = pl.pallas_call(
         functools.partial(kernel, groups, tokens, docs, length, chunks, vmem),
         out_shape=(jax.ShapeDtypeStruct((ROWS, dim), f32), jax.ShapeDtypeStruct((1, 1), f32)),
-        in_specs=[pl.BlockSpec(memory_space=pltpu.SMEM), VM, VM, pl.BlockSpec(memory_space=pl.ANY)],
+        in_specs=[pl.BlockSpec(memory_space=pl.ANY)] * 4,
         out_specs=(VM, VM),
         scratch_shapes=[
+            pltpu.SMEM((groups * ROWS,), jnp.int32),
+            pltpu.VMEM((ROWS, dim), bf16),
+            pltpu.VMEM((1, docs), jnp.int32),
             pltpu.VMEM((2 * groups, rows, lanes), bf16),
             pltpu.VMEM((rows, dim), bf16),
             pltpu.VMEM((dim, rows), bf16),
@@ -320,6 +335,7 @@
             pltpu.VMEM((groups * tokens, ROWS, dim), bf16),
             pltpu.VMEM((groups * tokens, ROWS, dim), bf16),
             pltpu.VMEM((groups * groups, ROWS, dim), f32),
+            DMA((3,)),
             DMA((chunks,)),
             DMA((groups,)),
             DMA((2 * groups,)),

time: 54.7 us -> 53.7 us (0.982)
  Pallas kernels: 50.3 us -> 49.1 us
    pallas_call x1, Pallas kernels: 50.3 us -> 49.1 us  [on_device(): pl.pallas_call(functools.partial(kernel, groups, tokens, docs, length, ch...]
where the time goes in v7:
time: 53.7 us; the launch traced here: 52.8 us
  Pallas kernels  49.1 us (91%)
  between operations  2.4 us (4%)
  local copies, waits for them, and re-layouts  1.3 us (2%)
    pallas_call x1, Pallas kernels, on_device(): pl.pallas_call(functools.partial(kernel, groups, tokens, docs, length, ch...  49.1 us
    unnamed x1, local copies, waits for them, and re-layouts  1.3 us

profile of v7, /device:TPU:1, one launch (start us, length us, event | category | flops | bytes accessed | tf_op | source)
XLA Modules:
  0.0 52.8 jit_solution(605495006780393728)
XLA Ops:
  0.6 49.1 %shard_map.59 = (f32[16,128]{1,0:T(8,128)}, f32[1,1]{1,0:T(1,128)}) custom-call(s32[64]{0:T(128)} %pos_in.1, bf16[16,128]{1,0:T(8,128)(2,1)} %bitcast.7, s32[1,128]{1,0:T(1,128)} %bitcast.8, bf16[12288,128]{1,0:T(8,128)(2,1)} %bitcast.5), custom_call_target="tpu_custom_call" | custom-call | tf_op jit(solution)/shard_map/pallas_call | solution.py:317
  50.3 1.3 %copy.9 = f32[1,16,128]{2,1,0:T(8,128)} copy(f32[1,16,128]{2,1,0:T(8,128)} %bitcast.6) | data formatting | bytes 16384

commit v8 on v7

--- a/solution.py
+++ b/solution.py
@@ -32,8 +32,8 @@
     groups, tokens, docs, length, chunks, vmem,
     pos_in, q_in, slot_in, queue_ref,
     grad_ref, loss_ref,
-    pos_ref, q_ref, slot_ref, powered, doc, doc_t, qbuf, sums, logits, slot_col, stats, fin, gsend, grecv, yrecv,
-    small_sem, load_sem, qy_recv, q_recv, s_recv, g_recv, y_recv, send_sem,
+    pos_ref, q_ref, slot_ref, powered, doc, doc_t, qbuf, sums, logits, slot_col, st1, st2, stats, fin, gsend, grecv, yrecv,
+    small_sem, load_sem, qy_recv, q_recv, s1_recv, s2_recv, s_recv, g_recv, y_recv, send_sem,
 ):
     group = lax.axis_index("group")
     me = lax.axis_index("queue")
@@ -45,6 +45,10 @@
     block_rows = rows // blocks
     block_docs = docs // blocks
     everyone = groups * tokens
+    early = groups - 2
+    few = 2 * groups
+    chips = tokens // 2
+    core = lax.rem(me, 2)
 
     def load(c):
         part = pl.ds(c * chunk, chunk)
@@ -175,23 +179,50 @@
         target = jnp.sum(jnp.where(hits(g), total, 0.0), axis=0, keepdims=True)
         row = jnp.where(field == 0, top, 0.0)
         row = jnp.where(field == 4, mass, row)
-        stats[g * everyone + group * tokens + me] = jnp.where(field == 5, target, row)
+        st1[g * few + group * 2 + core] = jnp.where(field == 5, target, row)
 
     def send_stats(g):
-        block = stats.at[g * everyone + group * tokens + me]
+        block = st1.at[g * few + group * 2 + core]
+        for i in range(groups):
+            for j in range(2):
+                if i + j > 0:
+                    pltpu.make_async_remote_copy(
+                        src_ref=block, dst_ref=block, send_sem=send_sem.at[1], recv_sem=s1_recv.at[g],
+                        device_id=(other_group(i), me + j * (1 - 2 * core)), device_id_type=MESH,
+                    ).start()
+
+    def combine(parts):
+        parts = parts.reshape(parts.shape[0], 128)
+        top = jnp.max(parts, axis=0, keepdims=True)
+        scale = jnp.exp(pltpu.roll(parts, 64, 1) - pltpu.roll(top, 64, 1))
+        return jnp.where(field < 4, top, jnp.sum(parts * scale, axis=0, keepdims=True))
+
+    def combine_column(g):
+        wait_in(st1.at[pl.ds(0, few - 1)], s1_recv.at[g])
+        row = g * chips + lax.div(me, 2)
+        st2[row] = combine(st1[pl.ds(g * few, few)])
+        block = st2.at[row]
+        for j in range(1, chips):
+            to_peer(block, block, send_sem.at[2], s2_recv.at[g], peer_of(2 * j)).start()
+
+    def combine_plane(g):
+        wait_in(st2.at[pl.ds(0, chips - 1)], s2_recv.at[g])
+        fin[g] = combine(st2[pl.ds(g * chips, chips)])
+
+    def send_all(g):
+        row = (g - early) * everyone + group * tokens + me
+        stats[row] = st1[g * few + group * 2 + core]
+        block = stats.at[row]
         steps = [(i, j) for i in range(groups) for j in range(tokens) if i + j > 0]
         for i, j in sorted(steps, key=lambda s: hops(s[1]) + min(s[0], groups - s[0]), reverse=True):
             pltpu.make_async_remote_copy(
-                src_ref=block, dst_ref=block, send_sem=send_sem.at[1], recv_sem=s_recv.at[g],
+                src_ref=block, dst_ref=block, send_sem=send_sem.at[5], recv_sem=s_recv.at[g - early],
                 device_id=(other_group(i), peer_of(j)), device_id_type=MESH,
             ).start()
 
-    def combine(g):
-        wait_in(stats.at[pl.ds(0, everyone - 1)], s_recv.at[g])
-        parts = stats[pl.ds(g * everyone, everyone)].reshape(everyone, 128)
-        top = jnp.max(parts, axis=0, keepdims=True)
-        scale = jnp.exp(pltpu.roll(parts, 64, 1) - pltpu.roll(top, 64, 1))
-        fin[g] = jnp.where(field < 4, top, jnp.sum(parts * scale, axis=0, keepdims=True))
+    def combine_all(g):
+        wait_in(stats.at[pl.ds(0, everyone - 1)], s_recv.at[g - early])
+        fin[g] = combine(stats[pl.ds((g - early) * everyone, everyone)])
 
     def wait_near(t):
         wait_in(qbuf.at[pl.ds(0, half - 1)], q_recv.at[t])
@@ -222,6 +253,11 @@
         send_stats(before)
         dots(2 * g)
         dots(2 * g + 1)
+
+        @pl.when(k == groups - 2)
+        def _():
+            combine_column(jnp.int32(0))
+
         return carry
 
     lax.fori_loop(0, 2, own_tile, 0)
@@ -229,6 +265,9 @@
     final = first_order(jnp.int32(groups - 1), group)
     scores(final)
     send_stats(final)
+    combine_column(jnp.int32(1))
+    send_all(early)
+    send_all(early + 1)
 
     def gradient(t, c):
         c = jnp.concatenate([c] * (lanes // 128), axis=1) / sums[t]
@@ -260,7 +299,15 @@
     def pass_b(k, carry):
         g = last_order(k, pivot, groups)
 
-        combine(g)
+
+        @pl.when(g < early)
+        def _():
+            combine_plane(g)
+
+        @pl.when(g >= early)
+        def _():
+            combine_all(g)
+
         row = fin[g]
         lse = everywhere(jnp.where(field == 0, row + jnp.log(pltpu.roll(row, 64, 1)), 0.0))
         c = (jnp.exp(logits[g] - lse) - hits(g).astype(jnp.float32)) / softness_divisor
@@ -296,9 +343,13 @@
     along = jnp.sum(q_unit * grad, axis=-1, keepdims=True)
     grad_ref[...] = (grad - q_unit * along) / q_length
 
+    for g in range(early, groups):
+        wait_in(st1.at[pl.ds(0, few - 1)], s1_recv.at[g])
     many = groups * (tokens - 1)
     wait_out(qbuf.at[pl.ds(0, many + groups - 1)], send_sem.at[0])
-    wait_out(stats.at[pl.ds(0, groups * (everyone - 1))], send_sem.at[1])
+    wait_out(st1.at[pl.ds(0, groups * (few - 1))], send_sem.at[1])
+    wait_out(st2.at[pl.ds(0, early * (chips - 1))], send_sem.at[2])
+    wait_out(stats.at[pl.ds(0, 2 * (everyone - 1))], send_sem.at[5])
     wait_out(gsend.at[pl.ds(0, many)], send_sem.at[3])
     if groups > 1:
         wait_out(yrecv.at[pl.ds(0, groups - 1)], send_sem.at[4])
@@ -330,7 +381,9 @@
             pltpu.VMEM((2 * groups, docs, lanes), f32),
             pltpu.VMEM((groups, docs, 128), f32),
             pltpu.VMEM((docs, 128), f32),
-            pltpu.VMEM((groups * groups * tokens, 1, 128), f32),
+            pltpu.VMEM((groups * groups * 2, 1, 128), f32),
+            pltpu.VMEM((groups * (tokens // 2), 1, 128), f32),
+            pltpu.VMEM((2 * groups * tokens, 1, 128), f32),
             pltpu.VMEM((groups, 1, 128), f32),
             pltpu.VMEM((groups * tokens, ROWS, dim), bf16),
             pltpu.VMEM((groups * tokens, ROWS, dim), bf16),
@@ -341,8 +394,10 @@
             DMA((2 * groups,)),
             DMA((groups,)),
             DMA((groups,)),
+            DMA((2,)),
+            DMA((groups,)),
             DMA,
-            DMA((5,)),
+            DMA((6,)),
         ],
         compiler_params=pltpu.CompilerParams(
             collective_id=0, has_side_effects=True, vmem_limit_bytes=vmem

time: 53.7 us -> 52.7 us (0.981); the launches traced: 52.8 us -> 52.3 us
  no operation moved by 1% of the time
where the time goes in v8:
time: 52.7 us; the launch traced here: 52.3 us
  Pallas kernels  48.6 us (92%)
  between operations  2.4 us (5%)
  local copies, waits for them, and re-layouts  1.3 us (2%)
    pallas_call x1, Pallas kernels, on_device(): pl.pallas_call(functools.partial(kernel, groups, tokens, docs, length, ch...  48.6 us
    unnamed x1, local copies, waits for them, and re-layouts  1.3 us

profile of v8, /device:TPU:1, one launch (start us, length us, event | category | flops | bytes accessed | tf_op | source)
XLA Modules:
  0.0 52.3 jit_solution(11788808628612661475)
XLA Ops:
  0.6 48.6 %shard_map.59 = (f32[16,128]{1,0:T(8,128)}, f32[1,1]{1,0:T(1,128)}) custom-call(s32[64]{0:T(128)} %pos_in.1, bf16[16,128]{1,0:T(8,128)(2,1)} %bitcast.7, s32[1,128]{1,0:T(1,128)} %bitcast.8, bf16[12288,128]{1,0:T(8,128)(2,1)} %bitcast.5), custom_call_target="tpu_custom_call" | custom-call | tf_op jit(solution)/shard_map/pallas_call | solution.py:368
  49.9 1.3 %copy.9 = f32[1,16,128]{2,1,0:T(8,128)} copy(f32[1,16,128]{2,1,0:T(8,128)} %bitcast.6) | data formatting | bytes 16384

commit v9 on v8

--- a/solution.py
+++ b/solution.py
@@ -263,9 +263,9 @@
     lax.fori_loop(0, 2, own_tile, 0)
     lax.fori_loop(1, groups, pass_a, 0)
     final = first_order(jnp.int32(groups - 1), group)
+    combine_column(jnp.int32(1))
     scores(final)
     send_stats(final)
-    combine_column(jnp.int32(1))
     send_all(early)
     send_all(early + 1)
 

time: 52.7 us -> 52.7 us (level)
  no operation moved by 1% of the time
where the time goes in v9:
time: 52.7 us; the launch traced here: 52.3 us
  Pallas kernels  48.6 us (92%)
  between operations  2.4 us (5%)
  local copies, waits for them, and re-layouts  1.3 us (2%)
    pallas_call x1, Pallas kernels, on_device(): pl.pallas_call(functools.partial(kernel, groups, tokens, docs, length, ch...  48.6 us
    unnamed x1, local copies, waits for them, and re-layouts  1.3 us

profile of v9, /device:TPU:1, one launch (start us, length us, event | category | flops | bytes accessed | tf_op | source)
XLA Modules:
  0.0 52.3 jit_solution(6309356280903191621)
XLA Ops:
  0.6 48.6 %shard_map.59 = (f32[16,128]{1,0:T(8,128)}, f32[1,1]{1,0:T(1,128)}) custom-call(s32[64]{0:T(128)} %pos_in.1, bf16[16,128]{1,0:T(8,128)(2,1)} %bitcast.7, s32[1,128]{1,0:T(1,128)} %bitcast.8, bf16[12288,128]{1,0:T(8,128)(2,1)} %bitcast.5), custom_call_target="tpu_custom_call" | custom-call | tf_op jit(solution)/shard_map/pallas_call | solution.py:368
  49.9 1.3 %copy.9 = f32[1,16,128]{2,1,0:T(8,128)} copy(f32[1,16,128]{2,1,0:T(8,128)} %bitcast.6) | data formatting | bytes 16384
